TPU v7x, 32 devices: a whole 2x2x4 slice. The times are simulated.
32 devices in a mesh: survey: 2 (over y), slab: 16 (over z, x, core).
Axes of the slice: x: 2, y: 2, z: 4, core: 2. Of those that a mesh axis runs over, the one named last changes fastest.
Arguments:
- cond: float32 [128, 128, 128], P(('survey', 'slab')), parts along dimension 0, may hold values from 0.3 to 3
- currents: float32 [2, 1024], P('survey'), parts along dimension 0, may hold values from -24 to 24
- source_planes: int32 [2, 1024], P('survey'), parts along dimension 0, may hold values from 0 to 63
- source_spots: int32 [2, 1024], P('survey'), parts along dimension 0, may hold values from 0 to 16383
- data: float32 [2, 2048], P('survey'), parts along dimension 0, may hold values from -6 to 6
- receiver_planes: int32 [2, 2048], P('survey'), parts along dimension 0, may hold values from 0 to 63
- receiver_spots: int32 [2, 2048], P('survey'), parts along dimension 0, may hold values from 0 to 16383
Outputs:
- potential: float32 [2, 64, 128, 128], P('survey', 'slab'), parts along dimension 0
- gradient: float32 [128, 128, 128], P(('survey', 'slab')), parts along dimension 0
There are 2 independent parts, one for each index of `survey`. A program takes and returns all parts, laid end to end along the dimension named above; each array names one. Nothing has to cross between parts.
Inputs may be any that keep to these rules, and one draw needn't show every extreme that they name: `source_planes`: entries may repeat. `receiver_planes`: entries may repeat.
All inputs are finite; a program needn't handle non-finite values.
Results may differ from a plain program's by a relative error of at most 0.0003.
Values sent between devices are 32-bit elements; how exact they have to be, the bound alone decides.
A program may use at most 64 MiB of HBM per device.

v0:
```python
import functools

import jax
import jax.numpy as jnp
import numpy as np
from jax import lax
from jax.experimental import pallas as pl
from jax.experimental.pallas import tpu as pltpu
from jax.sharding import PartitionSpec as P

DEPTH = 4
SIDE = 128
COARSE = 32
BF16 = jnp.bfloat16
F32 = jnp.float32
NT = (((1,), (1,)), ((), ()))


def split_np(table, axis, lead):
    high = table.astype(jnp.bfloat16)
    low = (table - high.astype(np.float64)).astype(jnp.bfloat16)
    return np.concatenate([high, high, low], axis=axis)


def tables(n):
    order = np.arange(COARSE, dtype=np.float64) + 1.0
    sine = np.sqrt(2.0 / (COARSE + 1.0)) * np.sin(
        np.pi * order[:, None] * order[None, :] / (COARSE + 1.0)
    )
    fine = np.repeat(sine, 4, axis=1)
    forward_y = split_np(fine, 1, 0)
    forward_z = split_np(np.tile(fine.T, (1, 4)), 0, 0)
    inverse_z = split_np(np.tile(fine, (4, 1)), 0, 0)
    inverse_y = split_np(fine.T, 1, 0)
    roots = 2.0 - 2.0 * np.cos(np.pi * order / (COARSE + 1.0))
    half = (2.0 + roots[:, None] + roots[None, :]) / 2.0
    theta = np.arccosh(half)
    scale = 1.0 / (
        16.0 * 2.0 * np.sinh(theta) * (-np.expm1(-(2.0 * n + 2.0) * theta))
    )
    pack = lambda a: a.reshape(4, 8, COARSE).transpose(1, 0, 2).reshape(8, SIDE)
    modes = np.stack([pack(theta), pack(scale)]).astype(np.float32)
    return forward_y, forward_z, inverse_z, inverse_y, modes


def pieces(value, axis):
    high = value.astype(BF16)
    low = (value - high.astype(F32)).astype(BF16)
    return jnp.concatenate([high, low, high], axis=axis)


def dot(a, b, dims=(((1,), (0,)), ((), ()))):
    return lax.dot_general(a, b, dims, preferred_element_type=F32)


def kernel(
    n,
    cond_h, cur_h, sp_h, ss_h, dat_h, rp_h, rs_h, fy_h, fz_h, iz_h, iy_h, mode_h,
    zf_o, grad_o, scal_o,
    cond, cur, sp, ss, dat, rp, rs, fy, fz, iz, iy, mode,
    mask_s, mask_r, sx, sy, sz, dg, w, r, cnt, dd, x1, x2, ru, za, zfull, weight,
    spec_f, spec_d, spec_u, sum_a, sum_b,
    got_f, got_d, got_u, got_a, got_b,
    local_sem, halo_send, halo_recv, send_sem, recv_sem,
):
    me = lax.axis_index("slab")
    peers = n - 1

    def each(body):
        if n <= 16:
            for k in range(1, n):
                body(k)
        else:
            pl.loop(1, n)(body)

    def peer(k):
        return {"slab": lax.rem(me + k, n)}

    barrier = pltpu.get_barrier_semaphore()
    each(lambda k: pl.semaphore_signal(barrier, inc=1, device_id=peer(k)))

    small = [(cur_h, cur), (sp_h, sp), (ss_h, ss), (rp_h, rp), (rs_h, rs), (dat_h, dat),
             (fy_h, fy), (fz_h, fz), (iz_h, iz), (iy_h, iy), (mode_h, mode)]
    loads = [pltpu.make_async_copy(a, b, local_sem.at[i]) for i, (a, b) in enumerate(small)]
    loads.append(pltpu.make_async_copy(cond_h, cond.at[pl.ds(4, 4)], local_sem.at[11]))
    for load in loads:
        load.start()

    halo = [
        (pl.ds(0, 2), pl.ds(8, 2), me - 1),
        (pl.ds(2, 2), pl.ds(10, 2), me - 1),
        (pl.ds(2, 2), pl.ds(2, 2), me + 1),
        (pl.ds(0, 2), pl.ds(0, 2), me + 1),
    ]

    def halo_copy(i):
        source, target, device = halo[i]
        return pltpu.make_async_remote_copy(
            src_ref=cond_h.at[source], dst_ref=cond.at[target],
            send_sem=halo_send.at[i], recv_sem=halo_recv.at[i],
            device_id={"slab": device},
        )

    has_low = me > 0
    has_high = me < n - 1

    @pl.when(me == 0)
    def _():
        cond[0:4] = jnp.zeros((4, SIDE, SIDE), F32)

    @pl.when(me == n - 1)
    def _():
        cond[8:12] = jnp.zeros((4, SIDE, SIDE), F32)

    row_s = lax.broadcasted_iota(jnp.int32, (SIDE, 1), 0)

    def build(planes, spots, low, count, masks):
        key = (planes[...] - low) * SIDE + lax.shift_right_logical(spots[...], 7)
        for p in range(count):
            masks[p * SIDE:(p + 1) * SIDE, :] = jnp.where(
                row_s + p * SIDE == key, 1.0, 0.0
            ).astype(BF16)
        return row_s == (spots[...] & (SIDE - 1))

    for i in range(3):
        loads[i].wait()
    here = build(sp, ss, me * DEPTH - 3, 10, mask_s)
    high = cur[...].astype(BF16).astype(F32)
    low = cur[...] - high
    columns = jnp.concatenate(
        [jnp.where(here, high, 0.0).astype(BF16), jnp.where(here, low, 0.0).astype(BF16)], axis=0
    )

    pl.semaphore_wait(barrier, peers)

    @pl.when(has_low)
    def _():
        halo_copy(0).start()

    @pl.when(has_high)
    def _():
        halo_copy(2).start()

    @pl.when(has_low)
    def _():
        halo_copy(1).start()

    @pl.when(has_high)
    def _():
        halo_copy(3).start()

    placed = dot(mask_s[...], columns, NT)
    for p in range(10):
        rows = slice(p * SIDE, (p + 1) * SIDE)
        r[p + 1] = placed[rows, 0:SIDE] + placed[rows, SIDE:2 * SIDE]

    for i in range(3, 6):
        loads[i].wait()
    here = build(rp, rs, me * DEPTH - 2, 8, mask_r)
    high = dat[...].astype(BF16).astype(F32)
    low = dat[...] - high
    columns = jnp.concatenate(
        [jnp.where(here, value, 0.0).astype(BF16) for value in (1.0, high, low)], axis=0
    )
    placed = dot(mask_r[...], columns, NT)
    for p in range(8):
        rows = slice(p * SIDE, (p + 1) * SIDE)
        cnt[p + 2] = placed[rows, 0:SIDE]
        dd[p + 2] = placed[rows, SIDE:2 * SIDE] + placed[rows, 2 * SIDE:3 * SIDE]

    for i in range(6, 12):
        loads[i].wait()

    def weigh(k):
        theta, scale = mode[0], mode[1]
        other = me - k
        other = jnp.where(other < 0, other + n, other)
        for t in range(3):
            mine = me + (t - 1)
            lower = jnp.minimum(mine, other)
            upper = jnp.maximum(mine, other)
            between = (upper - lower).astype(F32)
            below = (2 * (lower + 1)).astype(F32)
            above = (2 * (n - upper)).astype(F32)
            weight[t, k] = (
                scale
                * jnp.exp(-theta * between)
                * (1.0 - jnp.exp(-theta * below))
                * (1.0 - jnp.exp(-theta * above))
            )

    weigh(0)
    each(weigh)

    y_at = lax.broadcasted_iota(jnp.int32, (SIDE, SIDE), 0)
    z_at = lax.broadcasted_iota(jnp.int32, (SIDE, SIDE), 1)
    y_first, y_last = y_at == 0, y_at == SIDE - 1
    z_first, z_last = z_at == 0, z_at == SIDE - 1

    def back(v, axis):
        return pltpu.roll(v, 1, axis)

    def ahead(v, axis):
        return pltpu.roll(v, SIDE - 1, axis)

    def face_x(p):
        sx[p] = 0.5 * (cond[p - 1] + cond[p])

    def cell(p):
        c = cond[p]
        half = 0.5 * c
        prev_y = jnp.where(y_first, 0.0, back(half, 0))
        next_y = jnp.where(y_last, 0.0, ahead(half, 0))
        prev_z = jnp.where(z_first, 0.0, back(half, 1))
        next_z = jnp.where(z_last, 0.0, ahead(half, 1))
        sy[p] = jnp.where(y_first, 0.0, half + prev_y)
        sz[p] = jnp.where(z_first, 0.0, half + prev_z)
        total = sx[p] + sx[p + 1] + (c + prev_y + next_y) + (c + prev_z + next_z)
        if 4 <= p < 8:
            dg[p - 4] = total
            w[p] = (2.0 / 3.0) / total
        else:
            inside = has_low if p < 4 else has_high
            keep = jnp.where(inside, F32(1.0), F32(0.0))
            w[p] = keep * (2.0 / 3.0) / (total + (1.0 - keep))

    def around(v, p):
        mid = v[p]
        in_y, in_z = sy[p], sz[p]
        return (
            sx[p] * v[p - 1] + sx[p + 1] * v[p + 1]
            + (in_y * back(mid, 0) + ahead(in_y * mid, 0))
            + (in_z * back(mid, 1) + ahead(in_z * mid, 1))
        )

    lane_group = lax.broadcasted_iota(jnp.int32, (8, SIDE), 1) // COARSE

    def to_modes(field):
        left = dot(fy[...], pieces(field, 0))
        full = dot(pieces(left, 1), fz[...])
        out = jnp.zeros((8, SIDE), F32)
        for q in range(4):
            out = jnp.where(lane_group == q, full[8 * q:8 * q + 8], out)
        return out

    def from_modes(packed):
        rows = [jnp.where(lane_group == q, one, 0.0) for one in packed for q in range(4)]
        right = dot(pieces(jnp.concatenate(rows, axis=0), 1), iz[...])
        wide = jnp.concatenate([right[COARSE * t:COARSE * (t + 1)] for t in range(3)], axis=1)
        full = dot(iy[...], pieces(wide, 0))
        return [full[:, SIDE * t:SIDE * (t + 1)] for t in range(3)]

    def gather(source, target, number):
        def send(k):
            pltpu.make_async_remote_copy(
                src_ref=source, dst_ref=target.at[k - 1],
                send_sem=send_sem.at[number], recv_sem=recv_sem.at[number],
                device_id=peer(k),
            ).start()

        each(send)

    def arrived(target, number):
        pltpu.make_async_copy(target, target, recv_sem.at[number]).wait()

    def combine(own, target):
        def add(k, total):
            value = target[k - 1]
            return tuple(total[t] + weight[t, k] * value for t in range(3))

        total = tuple(weight[t, 0] * own[...] for t in range(3))
        if n <= 16:
            for k in range(1, n):
                total = add(k, total)
            return total
        return lax.fori_loop(1, n, add, total)

    def plane_of(p):
        return 0 if p < 4 else (1 if p < 8 else 2)

    @pl.when(has_high)
    def _():
        halo_copy(0).wait_recv()

    @pl.when(has_low)
    def _():
        halo_copy(2).wait_recv()

    for p in range(3, 10):
        face_x(p)
    for p in range(3, 9):
        cell(p)
        x1[p] = w[p] * r[p]
    total = None
    for p in range(4, 8):
        part = r[p] * (1.0 / 3.0) + around(x1, p)
        total = part if total is None else total + part
    spec_f[...] = to_modes(total)
    gather(spec_f, got_f, 0)

    for p in range(3, 9):
        x2[p] = w[p] * dd[p]
    total = None
    for p in range(4, 8):
        part = dd[p] * (1.0 / 3.0) + around(x2, p)
        total = part if total is None else total + part
    spec_d[...] = to_modes(total)
    gather(spec_d, got_d, 1)

    @pl.when(has_high)
    def _():
        halo_copy(1).wait_recv()

    @pl.when(has_low)
    def _():
        halo_copy(3).wait_recv()

    for p in (1, 2, 10, 11):
        face_x(p)
    for p in (1, 2, 9, 10):
        cell(p)
        x1[p] = w[p] * r[p]

    arrived(got_f, 0)
    lifted = from_modes(combine(spec_f, got_f))
    for p in range(1, 11):
        x2[p] = x1[p] + lifted[plane_of(p)]
    for p in range(2, 10):
        z = x2[p] * (1.0 / 3.0) + w[p] * (r[p] + around(x2, p))
        zfull[p] = z
        u = cnt[p] * z
        ru[p] = u
        x1[p] = w[p] * u
    total = None
    for p in range(4, 8):
        part = ru[p] * (1.0 / 3.0) + around(x1, p)
        total = part if total is None else total + part
    spec_u[...] = to_modes(total)
    gather(spec_u, got_u, 2)

    def sums(v, source):
        along = bend = None
        for p in range(4, 8):
            z = v[p]
            a = source(p) * z
            b = z * (dg[p - 4] * z - around(v, p))
            along = a if along is None else along + a
            bend = b if bend is None else bend + b
        return jnp.concatenate(
            [jnp.sum(along, axis=0, keepdims=True), jnp.sum(bend, axis=0, keepdims=True)], axis=0
        )

    def ratio(own, target):
        every = own[...] + jnp.sum(target[...], axis=0)
        both = jnp.sum(every, axis=1, keepdims=True)
        return both[0:1] / both[1:2]

    sum_a[...] = sums(zfull, lambda p: r[p])
    gather(sum_a, got_a, 3)
    for p in range(4):
        zf_o[p] = zfull[p + 4]

    arrived(got_d, 1)
    modes_d = combine(spec_d, got_d)
    arrived(got_a, 3)
    alpha = ratio(sum_a, got_a)
    arrived(got_u, 2)
    modes_u = combine(spec_u, got_u)
    lifted = from_modes([alpha * modes_u[t] - modes_d[t] for t in range(3)])
    for p in range(2, 10):
        ra = alpha * ru[p] - dd[p]
        r[p] = ra
        x2[p] = w[p] * ra + lifted[plane_of(p)]
    for p in range(3, 9):
        za[p] = x2[p] * (1.0 / 3.0) + w[p] * (r[p] + around(x2, p))
    sum_b[...] = sums(za, lambda p: r[p])
    gather(sum_b, got_b, 4)

    def face_pairs(f, a, first, last, axis):
        step_f = f - jnp.where(first, 0.0, back(f, axis))
        step_a = a - jnp.where(first, 0.0, back(a, axis))
        product = step_f * step_a
        return product + jnp.where(last, f * a, ahead(product, axis))

    lower = (zfull[4] - zfull[3]) * (za[4] - za[3])
    for p in range(4, 8):
        f, a = zfull[p], za[p]
        upper = (zfull[p + 1] - f) * (za[p + 1] - a)
        grad_o[p - 4] = (
            lower + upper
            + face_pairs(f, a, y_first, y_last, 0)
            + face_pairs(f, a, z_first, z_last, 1)
        )
        lower = upper

    @pl.when(has_low)
    def _():
        halo_copy(0).wait_send()
        halo_copy(1).wait_send()

    @pl.when(has_high)
    def _():
        halo_copy(2).wait_send()
        halo_copy(3).wait_send()

    for number, target in enumerate((got_f, got_d, got_u, got_a)):
        pltpu.make_async_copy(target, target, send_sem.at[number]).wait()
    arrived(got_b, 4)
    beta = ratio(sum_b, got_b)
    at = lax.broadcasted_iota(jnp.int32, (8, SIDE), 0)
    scal_o[...] = jnp.where(at == 0, alpha, -0.5 * alpha * beta)
    pltpu.make_async_copy(got_b, got_b, send_sem.at[4]).wait()


def on_device(n, cond, *rest):
    elec, recv = rest[0].shape[1], rest[3].shape[1]
    consts = tables(n)
    cube = lambda count: pltpu.VMEM((count, SIDE, SIDE), F32)
    vreg = pltpu.VMEM((8, SIDE), F32)
    pair = pltpu.VMEM((2, SIDE), F32)
    field = jax.ShapeDtypeStruct((DEPTH, SIDE, SIDE), F32)
    scratch = (
        [cube(12)]
        + [pltpu.VMEM(a.shape, a.dtype) for a in rest]
        + [pltpu.VMEM(a.shape, a.dtype) for a in consts]
        + [pltpu.VMEM((10 * SIDE, elec), BF16), pltpu.VMEM((8 * SIDE, recv), BF16)]
        + [cube(12), cube(12), cube(12), cube(4)]
        + [cube(12)] * 9
        + [pltpu.VMEM((3, n, 8, SIDE), F32)]
        + [vreg] * 3 + [pair] * 2
        + [pltpu.VMEM((n - 1, 8, SIDE), F32)] * 3
        + [pltpu.VMEM((n - 1, 2, SIDE), F32)] * 2
        + [
            pltpu.SemaphoreType.DMA((12,)),
            pltpu.SemaphoreType.DMA((4,)),
            pltpu.SemaphoreType.DMA((4,)),
            pltpu.SemaphoreType.DMA((5,)),
            pltpu.SemaphoreType.DMA((5,)),
        ]
    )
    zf, grad, scal = pl.pallas_call(
        functools.partial(kernel, n),
        out_shape=(field, field, jax.ShapeDtypeStruct((8, SIDE), F32)),
        in_specs=[pl.BlockSpec(memory_space=pl.ANY)] * 12,
        out_specs=[pl.BlockSpec(memory_space=pltpu.VMEM)] * 3,
        scratch_shapes=scratch,
        compiler_params=pltpu.CompilerParams(
            collective_id=0, has_side_effects=True, vmem_limit_bytes=48 * 1024 * 1024
        ),
    )(cond, *rest, *[jnp.asarray(c) for c in consts])
    return (scal[0, 0] * zf)[None], scal[1, 0] * grad


def solution(mesh):
    in_specs = (P(("survey", "slab"), None, None),) + (P("survey", None),) * 6
    out_specs = (P("survey", "slab", None, None), P(("survey", "slab"), None, None))
    return jax.shard_map(
        functools.partial(on_device, mesh.shape["slab"]),
        mesh=mesh, in_specs=in_specs, out_specs=out_specs, check_vma=False,
    )
```

profile of v0, /device:TPU:0, one launch (start us, length us, event | category | flops | bytes accessed | tf_op | source)
XLA Modules:
  0.0 40.0 jit_solution(7374652112875812450)
XLA Ops:
  0.6 0.0 copy-start
  0.6 0.9 %copy-done = f32[4,128,128]{2,1,0:T(8,128)S(1)} copy-done((f32[4,128,128]{2,1,0:T(8,128)S(1)}, f32[4,128,128]{2,1,0:T(8,128)}, u32[]{:S(2)}) %copy-start) | copy-done | bytes 262168
  1.6 0.0 copy-start.1
  1.6 0.9 %copy-done.1 = bf16[384,128]{1,0:T(8,128)(2,1)S(1)} copy-done((bf16[384,128]{1,0:T(8,128)(2,1)S(1)}, bf16[384,128]{1,0:T(8,128)(2,1)}, u32[]{:S(2)}) %copy-start.1) | copy-done | bytes 98328
  2.5 0.0 copy-start.2
  2.5 0.9 %copy-done.2 = bf16[384,128]{1,0:T(8,128)(2,1)S(1)} copy-done((bf16[384,128]{1,0:T(8,128)(2,1)S(1)}, bf16[384,128]{1,0:T(8,128)(2,1)}, u32[]{:S(2)}) %copy-start.2) | copy-done | bytes 98328
  3.4 0.0 copy-start.3
  3.4 0.8 %copy-done.3 = bf16[128,96]{1,0:T(8,128)(2,1)S(1)} copy-done((bf16[128,96]{1,0:T(8,128)(2,1)S(1)}, bf16[128,96]{1,0:T(8,128)(2,1)}, u32[]{:S(2)}) %copy-start.3) | copy-done | bytes 24600
  4.1 0.0 copy-start.4
  4.1 0.7 %copy-done.4 = bf16[32,384]{1,0:T(8,128)(2,1)S(1)} copy-done((bf16[32,384]{1,0:T(8,128)(2,1)S(1)}, bf16[32,384]{1,0:T(8,128)(2,1)}, u32[]{:S(2)}) %copy-start.4) | copy-done | bytes 24600
  4.9 0.0 copy-start.5
  4.9 0.7 %copy-done.5 = f32[1,2048]{1,0:T(1,128)S(1)} copy-done((f32[1,2048]{1,0:T(1,128)S(1)}, f32[1,2048]{1,0:T(1,128)}, u32[]{:S(2)}) %copy-start.5) | copy-done | bytes 8216
  5.6 0.0 copy-start.6
  5.6 0.7 %copy-done.6 = s32[1,2048]{1,0:T(1,128)S(1)} copy-done((s32[1,2048]{1,0:T(1,128)S(1)}, s32[1,2048]{1,0:T(1,128)}, u32[]{:S(2)}) %copy-start.6) | copy-done | bytes 8216
  6.3 0.0 copy-start.7
  6.3 0.7 %copy-done.7 = s32[1,2048]{1,0:T(1,128)S(1)} copy-done((s32[1,2048]{1,0:T(1,128)S(1)}, s32[1,2048]{1,0:T(1,128)}, u32[]{:S(2)}) %copy-start.7) | copy-done | bytes 8216
  7.0 0.0 copy-start.8
  7.0 0.7 %copy-done.8 = f32[2,8,128]{2,1,0:T(8,128)S(1)} copy-done((f32[2,8,128]{2,1,0:T(8,128)S(1)}, f32[2,8,128]{2,1,0:T(8,128)}, u32[]{:S(2)}) %copy-start.8) | copy-done | bytes 8216
  7.7 0.0 copy-start.9
  7.7 0.7 %copy-done.9 = f32[1,1024]{1,0:T(1,128)S(1)} copy-done((f32[1,1024]{1,0:T(1,128)S(1)}, f32[1,1024]{1,0:T(1,128)}, u32[]{:S(2)}) %copy-start.9) | copy-done | bytes 4120
  8.3 0.0 copy-start.10
  8.3 0.7 %copy-done.10 = s32[1,1024]{1,0:T(1,128)S(1)} copy-done((s32[1,1024]{1,0:T(1,128)S(1)}, s32[1,1024]{1,0:T(1,128)}, u32[]{:S(2)}) %copy-start.10) | copy-done | bytes 4120
  9.0 0.0 copy-start.11
  9.0 0.7 %copy-done.11 = s32[1,1024]{1,0:T(1,128)S(1)} copy-done((s32[1,1024]{1,0:T(1,128)S(1)}, s32[1,1024]{1,0:T(1,128)}, u32[]{:S(2)}) %copy-start.11) | copy-done | bytes 4120
  9.7 27.1 %shard_map.131 = (f32[4,128,128]{2,1,0:T(8,128)S(1)}, f32[4,128,128]{2,1,0:T(8,128)S(1)}, f32[8,128]{1,0:T(8,128)S(1)}) custom-call(f32[4,128,128]{2,1,0:T(8,128)S(1)} %copy-done, f32[1,1024]{1,0:T(1,128)S(1)} %copy-done.9, s32[1,1024]{1,0:T(1,128)S(1)} %copy-done.10, s32[1,1024]{1,0:T(1,128)S(1)} %copy-done.11, f32[1,2048]{1,0:T(1,128)S(1)} %copy-done.5, ...), custom_call_target="tpu_custom_call" | custom-call | tf_op jit(solution)/shard_map/pallas_call | solution.py:441
  36.9 0.5 %fusion = (f32[1,1]{1,0:T(1,128)}, f32[1,1]{1,0:T(1,128)}) fusion(f32[8,128]{1,0:T(8,128)S(1)} %get-tuple-element.5), kind=kLoop, calls=%fused_computation.2 | loop fusion | bytes 16 | tf_op jit(solution)/shard_map/slice | solution.py:451
  37.4 1.4 %broadcast_multiply_fusion = f32[4,128,128]{2,1,0:T(8,128)} fusion(f32[4,128,128]{2,1,0:T(8,128)S(1)} %get-tuple-element.7, f32[]{:T(128)} %bitcast.2), kind=kLoop, calls=%fused_computation.1 | loop fusion | flops 65536 | bytes 524292 | tf_op jit(solution)/shard_map/mul | solution.py:451
  38.7 1.3 %multiply_bitcast_fusion = f32[1,4,128,128]{3,2,1,0:T(8,128)} fusion(f32[4,128,128]{2,1,0:T(8,128)S(1)} %get-tuple-element.6, f32[]{:T(128)} %bitcast), kind=kLoop, calls=%fused_computation | loop fusion | flops 65536 | bytes 524292 | tf_op jit(solution)/shard_map/broadcast_in_dim | solution.py:451
Async XLA Ops:
  0.6 1.0 %copy-start = (f32[4,128,128]{2,1,0:T(8,128)S(1)}, f32[4,128,128]{2,1,0:T(8,128)}, u32[]{:S(2)}) copy-start(f32[4,128,128]{2,1,0:T(8,128)} %cond_h.1) | copy-start | bytes 786436
  1.6 0.9 %copy-start.1 = (bf16[384,128]{1,0:T(8,128)(2,1)S(1)}, bf16[384,128]{1,0:T(8,128)(2,1)}, u32[]{:S(2)}) copy-start(bf16[384,128]{1,0:T(8,128)(2,1)} %constant.12.clone.iz_h) | copy-start | bytes 294916
  2.5 0.9 %copy-start.2 = (bf16[384,128]{1,0:T(8,128)(2,1)S(1)}, bf16[384,128]{1,0:T(8,128)(2,1)}, u32[]{:S(2)}) copy-start(bf16[384,128]{1,0:T(8,128)(2,1)} %constant.11.clone.fz_h) | copy-start | bytes 294916
  3.4 0.8 %copy-start.3 = (bf16[128,96]{1,0:T(8,128)(2,1)S(1)}, bf16[128,96]{1,0:T(8,128)(2,1)}, u32[]{:S(2)}) copy-start(bf16[128,96]{1,0:T(8,128)(2,1)} %constant.13.clone.iy_h) | copy-start | bytes 73732
  4.1 0.7 %copy-start.4 = (bf16[32,384]{1,0:T(8,128)(2,1)S(1)}, bf16[32,384]{1,0:T(8,128)(2,1)}, u32[]{:S(2)}) copy-start(bf16[32,384]{1,0:T(8,128)(2,1)} %constant.10.clone.fy_h) | copy-start | bytes 73732
  4.9 0.7 %copy-start.5 = (f32[1,2048]{1,0:T(1,128)S(1)}, f32[1,2048]{1,0:T(1,128)}, u32[]{:S(2)}) copy-start(f32[1,2048]{1,0:T(1,128)} %dat_h.1) | copy-start | bytes 24580
  5.6 0.7 %copy-start.6 = (s32[1,2048]{1,0:T(1,128)S(1)}, s32[1,2048]{1,0:T(1,128)}, u32[]{:S(2)}) copy-start(s32[1,2048]{1,0:T(1,128)} %rp_h.1) | copy-start | bytes 24580
  6.3 0.7 %copy-start.7 = (s32[1,2048]{1,0:T(1,128)S(1)}, s32[1,2048]{1,0:T(1,128)}, u32[]{:S(2)}) copy-start(s32[1,2048]{1,0:T(1,128)} %rs_h.1) | copy-start | bytes 24580
  7.0 0.7 %copy-start.8 = (f32[2,8,128]{2,1,0:T(8,128)S(1)}, f32[2,8,128]{2,1,0:T(8,128)}, u32[]{:S(2)}) copy-start(f32[2,8,128]{2,1,0:T(8,128)} %constant.14.clone.mode_h) | copy-start | bytes 24580
  7.7 0.7 %copy-start.9 = (f32[1,1024]{1,0:T(1,128)S(1)}, f32[1,1024]{1,0:T(1,128)}, u32[]{:S(2)}) copy-start(f32[1,1024]{1,0:T(1,128)} %cur_h.1) | copy-start | bytes 12292
  8.3 0.7 %copy-start.10 = (s32[1,1024]{1,0:T(1,128)S(1)}, s32[1,1024]{1,0:T(1,128)}, u32[]{:S(2)}) copy-start(s32[1,1024]{1,0:T(1,128)} %sp_h.1) | copy-start | bytes 12292
  9.0 0.7 %copy-start.11 = (s32[1,1024]{1,0:T(1,128)S(1)}, s32[1,1024]{1,0:T(1,128)}, u32[]{:S(2)}) copy-start(s32[1,1024]{1,0:T(1,128)} %ss_h.1) | copy-start | bytes 12292
where the time goes:
time: 40.6 us; the launch traced here: 40 us
  Pallas kernels  27.1 us (67%)
  local copies, waits for them, and re-layouts  9.58 us (24%)
  other arithmetic  2.65 us (7%)
  between operations  0.66 us (2%)
    pallas_call x1, Pallas kernels, on_device(): pl.pallas_call(functools.partial(kernel, n), out_shape=(field, field, jax...  27.1 us
    unnamed x24, local copies, waits for them, and re-layouts  9.07 us
    mul x1, other arithmetic, on_device(): return ((scal[0, 0] * zf)[None], scal[1, 0] * grad)  1.37 us
    broadcast_in_dim x1, other arithmetic, on_device(): return ((scal[0, 0] * zf)[None], scal[1, 0] * grad)  1.28 us

commit v1 on v0

--- a/solution.py
+++ b/solution.py
@@ -11,6 +11,7 @@
 DEPTH = 4
 SIDE = 128
 COARSE = 32
+VMEM_BYTES = 63 * 1024 * 1024
 BF16 = jnp.bfloat16
 F32 = jnp.float32
 NT = (((1,), (1,)), ((), ()))
@@ -56,12 +57,13 @@
 def kernel(
     n,
     cond_h, cur_h, sp_h, ss_h, dat_h, rp_h, rs_h, fy_h, fz_h, iz_h, iy_h, mode_h,
-    zf_o, grad_o, scal_o,
+    zf_h, grad_h, scal_h,
     cond, cur, sp, ss, dat, rp, rs, fy, fz, iz, iy, mode,
     mask_s, mask_r, sx, sy, sz, dg, w, r, cnt, dd, x1, x2, ru, za, zfull, weight,
+    grad_o, scal_o,
     spec_f, spec_d, spec_u, sum_a, sum_b,
     got_f, got_d, got_u, got_a, got_b,
-    local_sem, halo_send, halo_recv, send_sem, recv_sem,
+    local_sem, out_sem, halo_send, halo_recv, send_sem, recv_sem,
 ):
     me = lax.axis_index("slab")
     peers = n - 1
@@ -357,8 +359,12 @@
 
     sum_a[...] = sums(zfull, lambda p: r[p])
     gather(sum_a, got_a, 3)
-    for p in range(4):
-        zf_o[p] = zfull[p + 4]
+    stores = [
+        pltpu.make_async_copy(zfull.at[pl.ds(4, 4)], zf_h, out_sem.at[0]),
+        pltpu.make_async_copy(grad_o, grad_h, out_sem.at[1]),
+        pltpu.make_async_copy(scal_o, scal_h, out_sem.at[2]),
+    ]
+    stores[0].start()
 
     arrived(got_d, 1)
     modes_d = combine(spec_d, got_d)
@@ -392,6 +398,7 @@
             + face_pairs(f, a, z_first, z_last, 1)
         )
         lower = upper
+    stores[1].start()
 
     @pl.when(has_low)
     def _():
@@ -409,7 +416,32 @@
     beta = ratio(sum_b, got_b)
     at = lax.broadcasted_iota(jnp.int32, (8, SIDE), 0)
     scal_o[...] = jnp.where(at == 0, alpha, -0.5 * alpha * beta)
+    stores[2].start()
     pltpu.make_async_copy(got_b, got_b, send_sem.at[4]).wait()
+    for store in stores:
+        store.wait()
+
+
+def scale_kernel(zf, grad, scal, potential, gradient, held, ready, factors, load_sem, sem):
+    loads = [
+        pltpu.make_async_copy(scal, factors, load_sem.at[0]),
+        pltpu.make_async_copy(zf, held.at[pl.ds(0, DEPTH)], load_sem.at[1]),
+        pltpu.make_async_copy(grad, held.at[pl.ds(DEPTH, DEPTH)], load_sem.at[2]),
+    ]
+    for load in loads:
+        load.start()
+    loads[0].wait()
+    copies = []
+    for row, target in enumerate((potential.at[0], gradient)):
+        loads[row + 1].wait()
+        factor = jnp.broadcast_to(factors[row:row + 1, :], (SIDE, SIDE))
+        for p in range(DEPTH):
+            at = row * DEPTH + p
+            ready[at] = factor * held[at]
+            copies.append(pltpu.make_async_copy(ready.at[at], target.at[p], sem.at[at]))
+            copies[-1].start()
+    for copy in copies:
+        copy.wait()
 
 
 def on_device(n, cond, *rest):
@@ -427,11 +459,13 @@
         + [cube(12), cube(12), cube(12), cube(4)]
         + [cube(12)] * 9
         + [pltpu.VMEM((3, n, 8, SIDE), F32)]
+        + [cube(DEPTH), vreg]
         + [vreg] * 3 + [pair] * 2
         + [pltpu.VMEM((n - 1, 8, SIDE), F32)] * 3
         + [pltpu.VMEM((n - 1, 2, SIDE), F32)] * 2
         + [
             pltpu.SemaphoreType.DMA((12,)),
+            pltpu.SemaphoreType.DMA((3,)),
             pltpu.SemaphoreType.DMA((4,)),
             pltpu.SemaphoreType.DMA((4,)),
             pltpu.SemaphoreType.DMA((5,)),
@@ -442,13 +476,23 @@
         functools.partial(kernel, n),
         out_shape=(field, field, jax.ShapeDtypeStruct((8, SIDE), F32)),
         in_specs=[pl.BlockSpec(memory_space=pl.ANY)] * 12,
-        out_specs=[pl.BlockSpec(memory_space=pltpu.VMEM)] * 3,
+        out_specs=[pl.BlockSpec(memory_space=pl.ANY)] * 3,
         scratch_shapes=scratch,
         compiler_params=pltpu.CompilerParams(
-            collective_id=0, has_side_effects=True, vmem_limit_bytes=48 * 1024 * 1024
+            collective_id=0, has_side_effects=True, vmem_limit_bytes=VMEM_BYTES
         ),
     )(cond, *rest, *[jnp.asarray(c) for c in consts])
-    return (scal[0, 0] * zf)[None], scal[1, 0] * grad
+    return pl.pallas_call(
+        scale_kernel,
+        out_shape=(jax.ShapeDtypeStruct((1, DEPTH, SIDE, SIDE), F32), field),
+        in_specs=[pl.BlockSpec(memory_space=pl.ANY)] * 3,
+        out_specs=[pl.BlockSpec(memory_space=pl.ANY)] * 2,
+        scratch_shapes=[
+            cube(2 * DEPTH), cube(2 * DEPTH), vreg,
+            pltpu.SemaphoreType.DMA((3,)), pltpu.SemaphoreType.DMA((2 * DEPTH,)),
+        ],
+        compiler_params=pltpu.CompilerParams(vmem_limit_bytes=VMEM_BYTES),
+    )(zf, grad, scal)
 
 
 def solution(mesh):

time: 40.6 us -> 30.6 us (0.75)
  local copies, waits for them, and re-layouts: 9.58 us -> 0 us
  Pallas kernels: 27.1 us -> 29.8 us
  other arithmetic: 2.65 us -> 0 us
    unnamed x24 -> x0, local copies, waits for them, and re-layouts: 9.07 us -> none
    pallas_call x0 -> x1, Pallas kernels: none -> 1.83 us  [on_device(): pl.pallas_call(scale_kernel, out_shape=(jax.ShapeDtypeStruct((1, DEPTH, S...]
    mul x1 -> x0, other arithmetic: 1.37 us -> none  [on_device(): return ((scal[0, 0] * zf)[None], scal[1, 0] * grad)]
    broadcast_in_dim x1 -> x0, other arithmetic: 1.28 us -> none  [on_device(): return ((scal[0, 0] * zf)[None], scal[1, 0] * grad)]
    pallas_call x1, Pallas kernels: 27.1 us -> 27.9 us  [on_device(): pl.pallas_call(functools.partial(kernel, n), out_shape=(field, field, jax...]
    slice x1 -> x0, local copies, waits for them, and re-layouts: 0.52 us -> none  [on_device(): return ((scal[0, 0] * zf)[None], scal[1, 0] * grad)]
where the time goes in v1:
time: 30.6 us; the launch traced here: 30.4 us
  Pallas kernels  29.8 us (97%)
  between operations  0.64 us (2%)
    pallas_call x1, Pallas kernels, on_device(): pl.pallas_call(functools.partial(kernel, n), out_shape=(field, field, jax...  27.9 us
    pallas_call x1, Pallas kernels, on_device(): pl.pallas_call(scale_kernel, out_shape=(jax.ShapeDtypeStruct((1, DEPTH, S...  1.83 us

profile of v1, /device:TPU:0, one launch (start us, length us, event | category | flops | bytes accessed | tf_op | source)
XLA Modules:
  0.0 30.4 jit_solution(11303264765207952391)
XLA Ops:
  0.6 27.9 %shard_map.131 = (f32[4,128,128]{2,1,0:T(8,128)}, f32[4,128,128]{2,1,0:T(8,128)}, f32[8,128]{1,0:T(8,128)}) custom-call(f32[4,128,128]{2,1,0:T(8,128)} %cond_h.1, f32[1,1024]{1,0:T(1,128)} %cur_h.1, s32[1,1024]{1,0:T(1,128)} %sp_h.1, s32[1,1024]{1,0:T(1,128)} %ss_h.1, f32[1,2048]{1,0:T(1,128)} %dat_h.1, s32[1,2048]{1,0:T(1,128)} %rp_h.1, s32[1,2048]{1,0:T(1,128)} %rs_h.1, ...), custom_call_target="tpu_custom_call" | custom-call | tf_op jit(solution)/shard_map/pallas_call | solution.py:475
  28.6 1.8 %shard_map.132 = (f32[1,4,128,128]{3,2,1,0:T(8,128)}, f32[4,128,128]{2,1,0:T(8,128)}) custom-call(f32[4,128,128]{2,1,0:T(8,128)} %get-tuple-element.5.zf, f32[4,128,128]{2,1,0:T(8,128)} %get-tuple-element.6.grad, f32[8,128]{1,0:T(8,128)} %get-tuple-element.7.scal), custom_call_target="tpu_custom_call" | custom-call | tf_op jit(solution)/shard_map/pallas_call | solution.py:485
